TPU v7x, 32 devices: a whole 2x2x4 slice. The times are simulated.
32 devices in a mesh: layer: 8 (over y, x, core), row: 4 (over z).
Axes of the slice: x: 2, y: 2, z: 4, core: 2. Of those that a mesh axis runs over, the one named last changes fastest.
Arguments:
- green: bfloat16 [8, 8192, 8192], P('layer', 'row'), may hold values from -0.09375 to 0.09375
- source_traces: bfloat16 [8, 128, 8192], P('layer', None, 'row'), may hold values from -6 to 6
Outputs:
- traces: bfloat16 [8, 128, 8192], P('layer', None, 'row')
All inputs are finite; a program needn't handle non-finite values.
Results may differ from a plain program's by a relative error of at most 0.007.
Values may be sent and summed in bfloat16 or wider, within the bound.
A program may use at most 128 MiB of HBM per device.

v0:
```python
import functools

import jax
import jax.numpy as jnp
from jax import lax
from jax.experimental import pallas as pl
from jax.experimental.pallas import tpu as pltpu
from jax.sharding import PartitionSpec as P

ITERS = 4
MESH = pl.DeviceIdType.MESH


def block_order(z, i, R):
    flip = (2 * z) // R
    zz = flip * (R - 1 - z) + (1 - flip) * z
    lead = R - 1 - 2 * zz
    tail = (i - lead + R) // R
    j2 = i - lead + 2 * R
    odd = j2 % 2
    h = j2 // 2 - R
    c = (1 - tail) * (R - 1 - i) + tail * ((1 - odd) * (2 * zz - h) + odd * h)
    return flip * (R - 1 - c) + (1 - flip) * c


def kernel(L, R, NC, green, src, out, g, inc, tr, rx, tx, acc,
           g_sem, inc_send, inc_recv, tx_sem, rx_sem):
    T = ITERS
    K = src.shape[2]
    H = src.shape[1] // 2
    KC = K // NC
    l = lax.axis_index("layer")
    z = lax.axis_index("row")
    span = max(L - 1 - T, 0)

    def place(half, layer):
        return layer if half == 0 else L - 1 - layer

    def active(half, t, layer):
        p = place(half, layer) - t
        return jnp.logical_and(p >= 0, p <= span)

    def sends_on(half, t):
        if t == T:
            return None
        p = place(half, l)
        return jnp.logical_and(p + 1 < L, jnp.logical_and(p - t >= 0, p - t <= span))

    def rows(half):
        return pl.ds(half * H, H)

    def cols(n):
        if isinstance(n, int):
            return pl.ds(n * KC, KC)
        return pl.ds(pl.multiple_of(n * KC, KC), KC)

    def green_copy(c, n):
        return pltpu.make_async_copy(
            green.at[0, :, pl.ds(pl.multiple_of(c * K + n * KC, KC), KC)],
            g.at[c, n], g_sem.at[c, n])

    def layer_copy(half, t, n):
        step = 1 if half == 0 else -1
        source = src.at[0] if t == 0 else tr.at[t - 1]
        return pltpu.make_async_remote_copy(
            src_ref=source.at[rows(half), cols(n)],
            dst_ref=inc.at[t, rows(half), cols(n)],
            send_sem=inc_send.at[t, half, n], recv_sem=inc_recv.at[t, half, n],
            device_id={"layer": l + step}, device_id_type=MESH)

    def row_copy(t, c, half, n, slot, to):
        return pltpu.make_async_remote_copy(
            src_ref=tx.at[c, half, n], dst_ref=rx.at[t - 1, slot, half, n],
            send_sem=tx_sem.at[c, half, n], recv_sem=rx_sem.at[t - 1, slot, half, n],
            device_id={"row": to}, device_id_type=MESH)

    def start_green(q, carry):
        green_copy(block_order(z, q // NC, R), q % NC).start()
        return carry

    lax.fori_loop(0, R * NC, start_green, 0)

    barrier = pltpu.get_barrier_semaphore()
    near = [(z > 0, {"row": z - 1}), (z < R - 1, {"row": z + 1}),
            (l > 0, {"layer": l - 1}), (l < L - 1, {"layer": l + 1})]
    for there, who in near:
        @pl.when(there)
        def _():
            pl.semaphore_signal(barrier, inc=1, device_id=who, device_id_type=MESH)
    peers = sum((at + size - 1) // size + (2 * size - 2 - at) // size
                for at, size in ((z, R), (l, L)))
    pl.semaphore_wait(barrier, peers)

    for half in range(2):
        @pl.when(sends_on(half, 0))
        def _():
            for n in range(NC):
                layer_copy(half, 0, n).start()

    for half in range(2):
        @pl.when(place(half, l) == 0)
        def _():
            out[0, rows(half), :] = src[0, rows(half), :]

    for t in range(1, T + 1):
        on = [active(half, t, l) for half in range(2)]
        either = jnp.logical_or(on[0], on[1])

        for half in range(2):
            @pl.when(on[half])
            def _():
                for n in range(NC):
                    layer_copy(half, t - 1, n).wait_recv()

            @pl.when(jnp.logical_and(either, jnp.logical_not(on[half])))
            def _():
                inc[t - 1, rows(half), :] = jnp.zeros((H, K), inc.dtype)

        def body(q, carry):
            i = q // NC
            n = q % NC
            c = block_order(z, i, R)
            if t == 1:
                green_copy(c, n).wait()

            @pl.when(either)
            def _():
                acc[...] = jnp.dot(inc[t - 1], g[c, n], preferred_element_type=jnp.float32)

            def add_received(half, slot):
                row_copy(t, c, half, n, slot, z).wait_recv()
                acc[rows(half), :] += rx[t - 1, slot, half, n].astype(jnp.float32)

            for half in range(2):
                @pl.when(jnp.logical_and(on[half], c != z))
                def _():
                    @pl.when(jnp.logical_or(jnp.logical_and(c > z, z > 0),
                                            jnp.logical_and(c < z, z < R - 1)))
                    def _():
                        add_received(half, c)

                    if t > 1:
                        @pl.when(active(half, t - 1, l))
                        def _():
                            row_copy(t, c, half, n, c, z).wait_send()

                    tx[c, half, n] = acc[rows(half), :].astype(tx.dtype)

                    @pl.when(c > z)
                    def _():
                        row_copy(t, c, half, n, c, z + 1).start()

                    @pl.when(c < z)
                    def _():
                        last = (c + 1 - z + R) // R
                        row_copy(t, c, half, n, c + last * (R - c), z - 1).start()

                @pl.when(jnp.logical_and(on[half], c == z))
                def _():
                    @pl.when(z > 0)
                    def _():
                        add_received(half, z)

                    @pl.when(z < R - 1)
                    def _():
                        add_received(half, R)

                    new = (src[0, rows(half), cols(n)].astype(jnp.float32)
                           + acc[rows(half), :]).astype(tr.dtype)

                    @pl.when(place(half, l) >= t if t == T else place(half, l) == t)
                    def _():
                        out[0, rows(half), cols(n)] = new

                    if t < T:
                        tr[t - 1, rows(half), cols(n)] = new

                        @pl.when(sends_on(half, t))
                        def _():
                            layer_copy(half, t, n).start()
            return carry

        lax.fori_loop(0, R * NC, body, 0)

    for half in range(2):
        for t in range(T):
            @pl.when(sends_on(half, t))
            def _():
                for n in range(NC):
                    layer_copy(half, t, n).wait_send()

        @pl.when(place(half, l) > 0)
        def _():
            def drain(q, carry):
                c = q // NC

                @pl.when(c != z)
                def _():
                    row_copy(1, c, half, q % NC, c, z).wait_send()
                return carry

            lax.fori_loop(0, R * NC, drain, 0)


def solution(mesh):
    L, R = mesh.shape["layer"], mesh.shape["row"]
    T = ITERS

    def local(green, source_traces):
        _, H2, K = source_traces.shape
        H = H2 // 2
        M = green.shape[2]
        KC = min(512, K)
        NC = K // KC
        bf = jnp.bfloat16
        dma = pltpu.SemaphoreType.DMA
        return pl.pallas_call(
            functools.partial(kernel, L, R, NC),
            out_shape=jax.ShapeDtypeStruct(source_traces.shape, bf),
            in_specs=[pl.BlockSpec(memory_space=pl.ANY),
                      pl.BlockSpec(memory_space=pltpu.VMEM)],
            out_specs=pl.BlockSpec(memory_space=pltpu.VMEM),
            scratch_shapes=[
                pltpu.VMEM((R, NC, K, KC), bf),
                pltpu.VMEM((T, H2, K), bf),
                pltpu.VMEM((T - 1, H2, K), bf),
                pltpu.VMEM((T, R + 1, 2, NC, H, KC), bf),
                pltpu.VMEM((R, 2, NC, H, KC), bf),
                pltpu.VMEM((H2, KC), jnp.float32),
                dma((R, NC)),
                dma((T, 2, NC)),
                dma((T, 2, NC)),
                dma((R, 2, NC)),
                dma((T, R + 1, 2, NC)),
            ],
            compiler_params=pltpu.CompilerParams(
                collective_id=0, has_side_effects=True,
                vmem_limit_bytes=60 * 2**20),
            cost_estimate=pl.CostEstimate(
                flops=2 * T * H2 * K * M, bytes_accessed=2 * K * M, transcendentals=0),
        )(green, source_traces)

    return jax.shard_map(
        local,
        mesh=mesh,
        in_specs=(P("layer", "row", None), P("layer", None, "row")),
        out_specs=P("layer", None, "row"),
        check_vma=False,
    )
```

profile of v0, /device:TPU:4, one launch (start us, length us, event | category | flops | bytes accessed | tf_op | source)
XLA Modules:
  0.0 136.8 jit_solution(3768503986304505681)
XLA Ops:
  0.0 134.9 %shard_map.28 = bf16[1,128,2048]{2,1,0:T(8,128)(2,1)} custom-call(bf16[1,2048,8192]{2,1,0:T(8,128)(2,1)} %green.1, bf16[1,128,2048]{2,1,0:T(8,128)(2,1)} %src.1), custom_call_target="tpu_custom_call" | custom-call | flops 17179869184 | bytes 33554432 | tf_op jit(solution)/shard_map/pallas_call | solution.py:217
  134.9 1.9 %copy.4 = bf16[1,128,2048]{2,1,0:T(8,128)(2,1)} copy(bf16[1,128,2048]{2,1,0:T(8,128)(2,1)} %shard_map.28) | data formatting | bytes 1048576
where the time goes:
time: 137 us
  Pallas kernels  135 us (99%)
  local copies, waits for them, and re-layouts  1.88 us (1%)
    pallas_call x1, Pallas kernels, local(): pl.pallas_call(functools.partial(kernel, L, R, NC), out_shape=jax.ShapeDt...  135 us

commit v1 on v0

--- a/solution.py
+++ b/solution.py
@@ -23,8 +23,16 @@
     return flip * (R - 1 - c) + (1 - flip) * c
 
 
-def kernel(L, R, NC, green, src, out, g, inc, tr, rx, tx, acc,
-           g_sem, inc_send, inc_recv, tx_sem, rx_sem):
+def below(a, k, n):
+    return 1 - (a - k + n) // n
+
+
+def equal(a, k, n):
+    return below(a, k + 1, n) - below(a, k, n)
+
+
+def kernel(L, R, NC, green, src, out, g, inc, tr, rx, tx, acc, ry,
+           g_sem, inc_send, inc_recv, tx_sem, rx_sem, ry_send, ry_recv):
     T = ITERS
     K = src.shape[2]
     H = src.shape[1] // 2
@@ -45,6 +53,14 @@
             return None
         p = place(half, l)
         return jnp.logical_and(p + 1 < L, jnp.logical_and(p - t >= 0, p - t <= span))
+
+    relayed = L % 4 == 0 and L >= 8 and R >= 3
+    turn = (2 * l) // L
+    depth = turn * (L - 1 - l) + (1 - turn) * l
+    helper = below(depth, 2, L)
+    helped = below(depth, 4, L) - helper
+    mate = l + 2 - 4 * ((l // 2) % 2)
+    ends = ((0, 1), (R - 1, R - 2)) if relayed else ()
 
     def rows(half):
         return pl.ds(half * H, H)
@@ -74,6 +90,21 @@
             send_sem=tx_sem.at[c, half, n], recv_sem=rx_sem.at[t - 1, slot, half, n],
             device_id={"row": to}, device_id_type=MESH)
 
+    def to_relay(t, c, half, n):
+        return pltpu.make_async_remote_copy(
+            src_ref=tx.at[c, half, n], dst_ref=ry.at[t - 1, half, n],
+            send_sem=tx_sem.at[c, half, n], recv_sem=ry_recv.at[t - 1, half, n],
+            device_id={"layer": mate}, device_id_type=MESH)
+
+    def from_relay(t, half, n, slot, to):
+        return pltpu.make_async_remote_copy(
+            src_ref=ry.at[t - 1, half, n], dst_ref=rx.at[t - 1, slot, half, n],
+            send_sem=ry_send.at[t - 1, half, n], recv_sem=rx_sem.at[t - 1, slot, half, n],
+            device_id={"layer": mate, "row": to}, device_id_type=MESH)
+
+    def relays(half, t):
+        return jnp.logical_and(helper == 1, active(half, t, mate))
+
     def start_green(q, carry):
         green_copy(block_order(z, q // NC, R), q % NC).start()
         return carry
@@ -83,12 +114,17 @@
     barrier = pltpu.get_barrier_semaphore()
     near = [(z > 0, {"row": z - 1}), (z < R - 1, {"row": z + 1}),
             (l > 0, {"layer": l - 1}), (l < L - 1, {"layer": l + 1})]
+    peers = sum((at + size - 1) // size + (2 * size - 2 - at) // size
+                for at, size in ((z, R), (l, L)))
+    for end, beside in ends:
+        near += [(jnp.logical_and(helper + helped == 1, z == end), {"layer": mate}),
+                 (jnp.logical_and(helper == 1, z == end), {"layer": mate, "row": beside}),
+                 (jnp.logical_and(helped == 1, z == beside), {"layer": mate, "row": end})]
+        peers += ((2 * helper + helped) * equal(z, end, R) + helped * equal(z, beside, R))
     for there, who in near:
         @pl.when(there)
         def _():
             pl.semaphore_signal(barrier, inc=1, device_id=who, device_id_type=MESH)
-    peers = sum((at + size - 1) // size + (2 * size - 2 - at) // size
-                for at, size in ((z, R), (l, L)))
     pl.semaphore_wait(barrier, peers)
 
     for half in range(2):
@@ -127,6 +163,21 @@
             def _():
                 acc[...] = jnp.dot(inc[t - 1], g[c, n], preferred_element_type=jnp.float32)
 
+            if t < T:
+                for end, beside in ends:
+                    @pl.when(jnp.logical_and(q == (R - 1) * NC,
+                                             jnp.logical_and(helper == 1, z == end)))
+                    def _():
+                        def hand_on(m, carry):
+                            for half in range(2):
+                                @pl.when(relays(half, t))
+                                def _():
+                                    to_relay(t, 0, half, m).wait_recv()
+                                    from_relay(t, half, m, 1 if end == 0 else R, beside).start()
+                            return carry
+
+                        lax.fori_loop(0, NC, hand_on, 0)
+
             def add_received(half, slot):
                 row_copy(t, c, half, n, slot, z).wait_recv()
                 acc[rows(half), :] += rx[t - 1, slot, half, n].astype(jnp.float32)
@@ -146,11 +197,22 @@
 
                     tx[c, half, n] = acc[rows(half), :].astype(tx.dtype)
 
-                    @pl.when(c > z)
+                    aside = False
+                    if t < T:
+                        for end, beside in ends:
+                            aside = jnp.logical_or(aside, jnp.logical_and(
+                                helped == 1, jnp.logical_and(z == end, c == beside)))
+                    straight = jnp.logical_not(aside)
+                    if t < T and ends:
+                        @pl.when(aside)
+                        def _():
+                            to_relay(t, c, half, n).start()
+
+                    @pl.when(jnp.logical_and(straight, c > z))
                     def _():
                         row_copy(t, c, half, n, c, z + 1).start()
 
-                    @pl.when(c < z)
+                    @pl.when(jnp.logical_and(straight, c < z))
                     def _():
                         last = (c + 1 - z + R) // R
                         row_copy(t, c, half, n, c + last * (R - c), z - 1).start()
@@ -183,6 +245,13 @@
         lax.fori_loop(0, R * NC, body, 0)
 
     for half in range(2):
+        if ends:
+            for t in range(1, T):
+                @pl.when(jnp.logical_and(relays(half, t), jnp.logical_or(z == 0, z == R - 1)))
+                def _():
+                    for n in range(NC):
+                        from_relay(t, half, n, 1, 1).wait_send()
+
         for t in range(T):
             @pl.when(sends_on(half, t))
             def _():
@@ -227,11 +296,14 @@
                 pltpu.VMEM((T, R + 1, 2, NC, H, KC), bf),
                 pltpu.VMEM((R, 2, NC, H, KC), bf),
                 pltpu.VMEM((H2, KC), jnp.float32),
+                pltpu.VMEM((T - 1, 2, NC, H, KC), bf),
                 dma((R, NC)),
                 dma((T, 2, NC)),
                 dma((T, 2, NC)),
                 dma((R, 2, NC)),
                 dma((T, R + 1, 2, NC)),
+                dma((T - 1, 2, NC)),
+                dma((T - 1, 2, NC)),
             ],
             compiler_params=pltpu.CompilerParams(
                 collective_id=0, has_side_effects=True,

time: 137 us -> 131 us (0.956)
  Pallas kernels: 135 us -> 129 us
    pallas_call x1, Pallas kernels: 135 us -> 129 us  [local(): pl.pallas_call(functools.partial(kernel, L, R, NC), out_shape=jax.ShapeDt...]
where the time goes in v1:
time: 131 us; the launch traced here: 130 us
  Pallas kernels  129 us (98%)
  local copies, waits for them, and re-layouts  1.88 us (1%)
    pallas_call x1, Pallas kernels, local(): pl.pallas_call(functools.partial(kernel, L, R, NC), out_shape=jax.ShapeDt...  129 us

profile of v1, /device:TPU:4, one launch (start us, length us, event | category | flops | bytes accessed | tf_op | source)
XLA Modules:
  0.0 130.5 jit_solution(2129834939104559092)
XLA Ops:
  0.0 128.6 %shard_map.28 = bf16[1,128,2048]{2,1,0:T(8,128)(2,1)} custom-call(bf16[1,2048,8192]{2,1,0:T(8,128)(2,1)} %green.1, bf16[1,128,2048]{2,1,0:T(8,128)(2,1)} %src.1), custom_call_target="tpu_custom_call" | custom-call | flops 17179869184 | bytes 33554432 | tf_op jit(solution)/shard_map/pallas_call | solution.py:286
  128.6 1.9 %copy.4 = bf16[1,128,2048]{2,1,0:T(8,128)(2,1)} copy(bf16[1,128,2048]{2,1,0:T(8,128)(2,1)} %shard_map.28) | data formatting | bytes 1048576
